TPU v7x, 256 devices: a whole 4x4x8 slice. The times are simulated.
256 devices in a mesh: step: 2 (over core), head: 8 (over z), blk: 16 (over y, x).
Axes of the slice: x: 4, y: 4, z: 8, core: 2. Of those that a mesh axis runs over, the one named last changes fastest.
Arguments:
- states: float32 [2, 2048, 3072], P('step', ('head', 'blk')), may hold values from -6 to 6
- start: float32 [2048, 3072], P(('head', 'blk')), may hold values from -6 to 6
- w_qkv: bfloat16 [3072, 3, 3072], P('blk', None, 'head'), may hold values from -0.109375 to 0.109375
- w_out: bfloat16 [3072, 3072], P(('head', 'blk')), may hold values from -0.109375 to 0.109375
- q_gain: float32 [64], replicated, may hold values from 1.5 to 5
- k_gain: float32 [64], replicated, may hold values from 1.5 to 5
- mod_table: float32 [50, 9216], replicated, may hold values from -3 to 3
- step_index: int32 [2], P('step'), may hold values from 0 to 49
- coef_table: float32 [50], replicated, may hold values from 0.1 to 1
- coef_index: int32 [2], P('step'), may hold values from 0 to 49
Outputs:
- new_states: float32 [2, 2048, 3072], P('step', ('head', 'blk'))
All inputs are finite; a program needn't handle non-finite values.
Results may differ from a plain program's by a relative error of at most 0.008.
Values may be sent and summed in bfloat16 or wider, within the bound.
No kernel may reach another device: no remote copies, remote signals or barrier semaphores. Data moves between devices by JAX's collectives and lax.ppermute only.
A program may use at most 128 MiB of HBM per device.

v0:
```python
import jax
import jax.numpy as jnp
from jax import lax
from jax.sharding import PartitionSpec as P

HD = 64


def carried_in(array, axis, join, neutral):
    place = lax.axis_index(axis)
    gathered = lax.all_gather(array.astype(jnp.bfloat16), axis)
    state = jnp.zeros_like(array) + jnp.asarray(neutral, array.dtype)

    def one(step, state):
        return join(state, lax.dynamic_index_in_dim(gathered, step, 0, False).astype(array.dtype))

    return lax.fori_loop(0, place, one, state)


def head_norm(values_in, gains):
    middle = jnp.mean(values_in, axis=-1, keepdims=True)
    spread = jnp.mean((values_in - middle) ** 2, axis=-1, keepdims=True)
    return (values_in - middle) * lax.rsqrt(spread + 1e-06) * gains


def on_device(
    states, start, w_qkv, w_out, q_gain, k_gain, mod_table, step_index, coef_table, coef_index
):
    width = states.shape[2]
    table_size = mod_table.shape[0]
    slot_ids = jnp.arange(table_size, dtype=jnp.int32)[None, :]
    mod_picks = (step_index[:, None] == slot_ids).astype(jnp.float32)
    coef_picks = (coef_index[:, None] == slot_ids).astype(jnp.float32)
    modulation = jnp.dot(mod_picks, mod_table, precision=lax.Precision.HIGHEST).reshape(
        -1, 3, width
    )
    coefs = jnp.sum(coef_picks * coef_table[None, :], axis=1)
    middle = jnp.mean(states, axis=-1, keepdims=True)
    spread = jnp.mean((states - middle) ** 2, axis=-1, keepdims=True)
    normed = (
        (states - middle) * lax.rsqrt(spread + 1e-05) * (1.0 + modulation[:, 1][:, None, :])
        + modulation[:, 0][:, None, :]
    ).astype(jnp.bfloat16)
    weight_rows = lax.all_gather(w_qkv, "blk", axis=0, tiled=True)
    projected = jnp.einsum(
        "std,dce->stce",
        lax.all_gather(normed, "head", axis=1, tiled=True),
        weight_rows,
        preferred_element_type=jnp.float32,
    )
    step_count = projected.shape[0]
    row_count = projected.shape[1]
    local_heads = projected.shape[3] // HD
    queries = head_norm(
        projected[:, :, 0].reshape(step_count, row_count, local_heads, HD), q_gain
    ).astype(jnp.bfloat16)
    keys_here = head_norm(
        projected[:, :, 1].reshape(step_count, row_count, local_heads, HD), k_gain
    ).astype(jnp.bfloat16)
    values_here = (
        projected[:, :, 2].reshape(step_count, row_count, local_heads, HD).astype(jnp.bfloat16)
    )
    scale_factor = HD ** (-0.5)
    start_best = jnp.full((step_count, local_heads, row_count), -1e30, jnp.float32)
    start_totals = jnp.zeros((step_count, local_heads, row_count), jnp.float32)
    start_accum = jnp.zeros((step_count, local_heads, row_count, HD), jnp.float32)
    best = start_best
    totals = start_totals
    accum = start_accum
    key_piece = lax.all_gather(keys_here, "blk", axis=1, tiled=True)
    value_piece = lax.all_gather(values_here, "blk", axis=1, tiled=True)
    length = key_piece.shape[1]
    for offset in range(0, length, 512):
        stop = min(offset + 512, length)
        key_block = key_piece[:, offset:stop]
        value_block = value_piece[:, offset:stop]
        scores = (
            jnp.einsum("sqhd,skhd->shqk", queries, key_block, preferred_element_type=jnp.float32)
            * scale_factor
        )
        new_best = jnp.maximum(best, jnp.max(scores, axis=-1))
        factor = jnp.exp(best - new_best)
        weights = jnp.exp(scores - new_best[..., None])
        totals = totals * factor + jnp.sum(weights, axis=-1)
        accum = accum * factor[..., None] + jnp.einsum(
            "shqk,skhd->shqd",
            weights.astype(jnp.bfloat16),
            value_block,
            preferred_element_type=jnp.float32,
        )
        best = new_best
    best, totals, accum = (best, totals, accum)
    attn = jnp.transpose(accum / totals[..., None], (0, 2, 1, 3)).reshape(
        step_count, row_count, local_heads * HD
    )
    attn = attn.astype(jnp.bfloat16)
    group_terms = jnp.einsum(
        "srf,fe->sre",
        attn,
        lax.all_gather(w_out, "blk", axis=0, tiled=True),
        preferred_element_type=jnp.float32,
    )
    mixed = lax.psum_scatter(
        group_terms.astype(jnp.bfloat16), "head", scatter_dimension=1, tiled=True
    ).astype(jnp.float32)
    drift = modulation[:, 2][:, None, :] * mixed
    inclusive = jnp.cumsum(coefs[:, None, None] * drift, axis=0)
    own_total = inclusive[-1]
    earlier = carried_in(
        own_total, "step", lambda first, second: first + second, jnp.zeros_like(own_total)
    )
    return start[None] + (earlier[None] + inclusive)


def solution(mesh):
    in_specs = (
        P("step", ("head", "blk"), None),
        P(("head", "blk"), None),
        P("blk", None, "head"),
        P(("head", "blk"), None),
        P(),
        P(),
        P(),
        P("step"),
        P(),
        P("step"),
    )
    out_specs = P("step", ("head", "blk"), None)
    return jax.shard_map(
        on_device, mesh=mesh, in_specs=in_specs, out_specs=out_specs, check_vma=False
    )
```

profile of v0, /device:TPU:1, one launch (start us, length us, event | category | flops | bytes accessed | tf_op | source)
XLA Modules:
  0.0 296.6 jit_solution(17532198144011052119)
XLA Ops:
  6.5 0.0 all-gather.5.cloned.1.call-start
  6.5 0.7 all-gather.5.cloned.1.call-update
  7.3 0.0 all-gather.7.cloned.1.call-start
  7.3 0.0 copy-start.3
  7.3 3.2 %reshape.440 = f32[3,3072,50]{1,0,2:T(4,128)S(1)} reshape(f32[9216,50]{0,1:T(8,128)} %bitcast.98) | data formatting | bytes 3686400 | tf_op jit(solution)/shard_map/reshape.224
  11.1 0.0 copy-done.3
  11.2 0.1 reduce_sum.100
  11.3 0.2 multiply_reduce_fusion.2
  11.5 1.8 fusion.1
  13.4 0.1 add_convert_fusion
  13.5 25.1 %all_gather.19 = bf16[1,128,3072]{2,1,0:T(8,128)(2,1)S(1)} all-gather(bf16[1,16,3072]{2,1,0:T(8,128)(2,1)S(1)} %add_convert_fusion), channel_id=1, replica_groups=mesh['step'=2,'head'=8,'blk'=16] {'head'}, dimensions={1}, use_global_device_ids=true | all-gather | bytes 884736 | tf_op jit(solution)/shard_map/all_gather | solution.py:47
  38.6 45.0 %all-gather.5.cloned.1.call-done = bf16[3072,3,384]{2,0,1:T(8,128)(2,1)} async-done(((bf16[192,3,384]{2,0,1:T(8,128)(2,1)}), bf16[3072,3,384]{2,0,1:T(8,128)(2,1)}) %all-gather.5.cloned.1.call-update) | async-done | bytes 7077904 | tf_op jit(solution)/shard_map/all_gather | solution.py:44
  83.5 4.2 %convolution_bitcast_fusion = f32[1,128,3,384]{3,1,2,0:T(8,128)S(1)} fusion(bf16[3072,3,384]{2,0,1:T(8,128)(2,1)} %all-gather.5.cloned.1.call-done, bf16[1,128,3072]{2,1,0:T(8,128)(2,1)S(1)} %all_gather.19), kind=kOutput, calls=%fused_computation.21 | convolution fusion | flops 905969664 | bytes 8454144 | tf_op jit(solution)/shard_map/std,dce->stce/dot_general | solution.py:45
  87.8 0.0 copy-start.8
  87.8 0.0 copy-start.9
  87.8 0.1 copy.22
  88.0 0.4 copy-done.8
  88.4 0.7 multiply_convert_fusion
  89.1 0.0 all-gather.7.cloned.1.call-update
  89.2 0.0 all-gather.9.cloned.1.call-start
  89.2 0.7 copy.24
  90.0 0.0 all-gather.9.cloned.1.call-update
  90.0 0.0 all-gather.11.cloned.1.call-start
  90.0 0.5 all-gather.11.cloned.1.call-update
  90.6 0.0 reduce-scatter.2.cloned.1.call-start
  90.6 0.1 copy.20
  90.8 0.0 copy-done.9
  90.9 0.1 multiply_convert_fusion.1
  90.9 47.2 %all-gather.7.cloned.1.call-done = bf16[1,2048,6,64]{1,3,2,0:T(8,128)(2,1)} async-done(((bf16[1,128,6,64]{1,3,2,0:T(8,128)(2,1)}), bf16[1,2048,6,64]{1,3,2,0:T(8,128)(2,1)}) %all-gather.7.cloned.1.call-update) | async-done | bytes 1572880 | tf_op jit(solution)/shard_map/all_gather | solution.py:70
  138.2 0.0 copy-start.4
  138.2 1.6 fusion.41
  139.8 0.0 copy-done.4
  139.8 0.0 copy-start
  139.8 0.5 fusion.40
  140.3 0.5 fusion.39
  140.8 0.5 fusion.38
  141.3 0.0 copy-start.1
  141.3 0.0 copy-done
  141.3 0.9 fusion.3
  142.2 0.2 copy-done.1
  142.5 0.9 fusion.7
  143.4 47.1 %all-gather.9.cloned.1.call-done = bf16[1,2048,6,64]{1,3,2,0:T(8,128)(2,1)} async-done(((bf16[1,128,6,64]{1,3,2,0:T(8,128)(2,1)}), bf16[1,2048,6,64]{1,3,2,0:T(8,128)(2,1)}) %all-gather.9.cloned.1.call-update) | async-done | bytes 1572880 | tf_op jit(solution)/shard_map/all_gather | solution.py:71
  190.5 0.0 copy-start.5
  190.5 2.1 fusion.14
  192.5 0.0 copy-done.5
  192.5 0.5 fusion.13
  193.0 0.0 copy-start.2
  193.0 0.5 fusion.12
  193.5 0.9 copy-done.2
  194.4 0.5 fusion.15
  194.9 48.3 %all-gather.11.cloned.1.call-done = bf16[384,3072]{1,0:T(8,128)(2,1)} async-done(((bf16[24,3072]{1,0:T(8,128)(2,1)}), bf16[384,3072]{1,0:T(8,128)(2,1)}) %all-gather.11.cloned.1.call-update) | async-done | bytes 2359312 | tf_op jit(solution)/shard_map/all_gather | solution.py:100
  243.3 3.2 %fusion = bf16[1,128,3072]{2,1,0:T(8,128)(2,1)} fusion(bf16[128,384]{0,1:T(8,128)(2,1)S(1)} %bitcast.102, bf16[384,3072]{1,0:T(8,128)(2,1)} %all-gather.11.cloned.1.call-done), kind=kOutput, calls=%fused_computation.2 | convolution fusion | flops 302383104 | bytes 3244032 | tf_op jit(solution)/shard_map/srf,fe->sre/dot_general | solution.py:97
  246.4 0.0 reduce-scatter.2.cloned.1.call-update
  247.1 0.0 copy-done.10
  247.1 0.6 fusion.30
  247.7 32.7 %reduce-scatter.2.cloned.1.call-done = bf16[1,16,3072]{2,1,0:T(8,128)(2,1)} async-done(((bf16[1,128,3072]{2,1,0:T(8,128)(2,1)}), bf16[1,16,3072]{2,1,0:T(8,128)(2,1)}) %reduce-scatter.2.cloned.1.call-update) | async-done | bytes 98320 | tf_op jit(solution)/shard_map/reduce_scatter | solution.py:103
  280.4 1.5 fusion.26
  281.9 0.0 copy-start.6
  281.9 0.0 copy-start.7
  281.9 6.8 %all_gather.24 = bf16[2,16,3072]{2,1,0:T(8,128)(2,1)S(1)} all-gather(bf16[1,16,3072]{2,1,0:T(8,128)(2,1)S(1)} %fusion.26), channel_id=1, replica_groups=mesh['step'=2,'head'=8,'blk'=16] {'step'}, dimensions={0}, use_global_device_ids=true | all-gather | bytes 294912 | tf_op jit(solution)/shard_map/all_gather | solution.py:11
  288.7 0.1 while.10
  288.8 0.0 copy-done.6
  288.8 0.0 copy-done.7
  288.8 1.3 fusion.25
  (19 shorter events, 0.3 us)
Async XLA Ops:
  6.5 77.0 %all-gather.5.cloned.1.call-start = ((), (), s32[]{:S(2)}) async-start(), calls=%async_computation.1 | async-start | bytes 7520256 | tf_op jit(solution)/shard_map/all_gather | solution.py:44
  7.3 130.9 %all-gather.7.cloned.1.call-start = ((), (), s32[]{:S(2)}) async-start(), calls=%async_computation.2 | async-start | bytes 1671168 | tf_op jit(solution)/shard_map/all_gather | solution.py:70
  7.3 3.8 %copy-start.3 = (f32[1,16,3072]{2,1,0:T(8,128)S(1)}, f32[1,16,3072]{2,1,0:T(8,128)}, u32[]{:S(2)}) copy-start(f32[1,16,3072]{2,1,0:T(8,128)} %param.12) | copy-start | bytes 589828
  87.8 0.7 copy-start.8
  87.8 3.1 %copy-start.9 = (f32[64]{0:T(128)S(1)}, f32[64]{0:T(128)}, u32[]{:S(2)}) copy-start(f32[64]{0:T(128)} %param.16) | copy-start | bytes 772
  89.2 101.3 %all-gather.9.cloned.1.call-start = ((), (), s32[]{:S(2)}) async-start(), calls=%async_computation.3 | async-start | bytes 1671168 | tf_op jit(solution)/shard_map/all_gather | solution.py:71
  90.0 153.3 %all-gather.11.cloned.1.call-start = ((), (), s32[]{:S(2)}) async-start(), calls=%async_computation.4 | async-start | bytes 2506752 | tf_op jit(solution)/shard_map/all_gather | solution.py:100
  90.6 189.8 %reduce-scatter.2.cloned.1.call-start = ((), (), s32[]{:S(2)}) async-start(), calls=%async_computation.5 | async-start | bytes 884736 | tf_op jit(solution)/shard_map/reduce_scatter | solution.py:103
  138.2 1.6 copy-start.4
  139.8 1.5 copy-start
  141.3 1.2 copy-start.1
  190.5 2.1 copy-start.5
  193.0 1.4 copy-start.2
  243.3 3.9 %copy-start.10 = (f32[50]{0:T(128)S(1)}, f32[50]{0:T(128)}, u32[]{:S(2)}) copy-start(f32[50]{0:T(128)} %param.20) | copy-start | bytes 604
  281.9 6.9 %copy-start.6 = (bf16[1,16,3072]{2,1,0:T(8,128)(2,1)S(1)}, bf16[1,16,3072]{2,1,0:T(8,128)(2,1)}, u32[]{:S(2)}) copy-start(bf16[1,16,3072]{2,1,0:T(8,128)(2,1)} %reduce-scatter.2.cloned.1.call-done) | copy-start | bytes 294916
  281.9 6.9 %copy-start.7 = (f32[16,3072]{1,0:T(8,128)S(1)}, f32[16,3072]{1,0:T(8,128)}, u32[]{:S(2)}) copy-start(f32[16,3072]{1,0:T(8,128)} %param.13) | copy-start | bytes 589828
Sparse Core Ops, SparseCore 0:
  9.8 73.7 all-gather.4
  89.3 48.8 all-gather.6
  140.6 49.8 all-gather.8
  192.8 50.4 all-gather.10
  246.6 33.7 reduce-scatter.1
where the time goes:
time: 297 us
  waiting for transfers between devices  222 us (75%)
  blocking collectives  31.8 us (11%)
  matrix products  15.8 us (5%)
  between operations  14.8 us (5%)
  other arithmetic  6.61 us (2%)
  local copies, waits for them, and re-layouts  5.77 us (2%)
    all_gather x1, waiting for transfers between devices, on_device(): lax.all_gather(w_out, 'blk', axis=0, tiled=True)  48.3 us
    all_gather x1, waiting for transfers between devices, on_device(): key_piece = lax.all_gather(keys_here, 'blk', axis=1, tiled=True)  47.2 us
    all_gather x1, waiting for transfers between devices, on_device(): value_piece = lax.all_gather(values_here, 'blk', axis=1, tiled=True)  47.1 us
    all_gather x1, waiting for transfers between devices, on_device(): weight_rows = lax.all_gather(w_qkv, 'blk', axis=0, tiled=True)  45 us
    reduce_scatter x1, waiting for transfers between devices, on_device(): lax.psum_scatter(group_terms.astype(jnp.bfloat16), 'head', scatter_dimens...  32.7 us
    all_gather x1, blocking collectives, on_device(): lax.all_gather(normed, 'head', axis=1, tiled=True)  25.1 us
    all_gather x1, blocking collectives, carried_in(): gathered = lax.all_gather(array.astype(jnp.bfloat16), axis)  6.76 us
  transfers between devices with their start and end apart: 5, of which 5 were waited for; matrix products, arithmetic and copies ran while one was open for 5% of the time, Pallas kernels for 0%

commit v1 on v0

--- a/solution.py
+++ b/solution.py
@@ -1,9 +1,20 @@
+import functools
 import jax
 import jax.numpy as jnp
 from jax import lax
 from jax.sharding import PartitionSpec as P
 
 HD = 64
+
+
+def trees_build(arr_in, peer_axis):
+    opened = jnp.concatenate(
+        lax.all_to_all(jnp.stack(lax.axis_size(peer_axis) * [arr_in]), peer_axis, 0, 0), axis=0
+    )
+    return opened
+
+
+close_hubs_by_axis = functools.partial(trees_build, peer_axis="blk")
 
 
 def carried_in(array, axis, join, neutral):
@@ -41,7 +52,7 @@
         (states - middle) * lax.rsqrt(spread + 1e-05) * (1.0 + modulation[:, 1][:, None, :])
         + modulation[:, 0][:, None, :]
     ).astype(jnp.bfloat16)
-    weight_rows = lax.all_gather(w_qkv, "blk", axis=0, tiled=True)
+    weight_rows = close_hubs_by_axis(w_qkv)
     projected = jnp.einsum(
         "std,dce->stce",
         lax.all_gather(normed, "head", axis=1, tiled=True),

time: 297 us -> 341 us (1.15)
  waiting for transfers between devices: 222 us -> 249 us
  local copies, waits for them, and re-layouts: 5.77 us -> 14.7 us
  starting transfers between devices: 0.16 us -> 7.79 us
    all_to_all x0 -> x1, waiting for transfers between devices: none -> 71.2 us  [trees_build(): lax.all_to_all(jnp.stack(lax.axis_size(peer_axis) * [arr_in]), peer_axis,...]
    all_gather x1 -> x0, waiting for transfers between devices: 45 us -> none  [on_device(): weight_rows = lax.all_gather(w_qkv, 'blk', axis=0, tiled=True)]
    all_to_all x0 -> x1, starting transfers between devices: none -> 7.63 us  [trees_build(): lax.all_to_all(jnp.stack(lax.axis_size(peer_axis) * [arr_in]), peer_axis,...]
    another operation x1 -> x2, local copies, waits for them, and re-layouts: 3.17 us -> 8.24 us  [the longest x1 5.07 us: trees_build(): jnp.stack(lax.axis_size(peer_axis) * [arr_in])]
    all_to_all x0 -> x1, local copies, waits for them, and re-layouts: none -> 3.88 us  [trees_build(): lax.all_to_all(jnp.stack(lax.axis_size(peer_axis) * [arr_in]), peer_axis,...]
where the time goes in v1:
time: 341 us; the launch traced here: 340 us
  waiting for transfers between devices  249 us (73%)
  blocking collectives  33.6 us (10%)
  between operations  14.8 us (4%)
  local copies, waits for them, and re-layouts  14.7 us (4%)
  matrix products  13.4 us (4%)
  starting transfers between devices  7.79 us (2%)
  other arithmetic  6.95 us (2%)
    all_to_all x1, waiting for transfers between devices, trees_build(): lax.all_to_all(jnp.stack(lax.axis_size(peer_axis) * [arr_in]), peer_axis,...  71.2 us
    all_gather x1, waiting for transfers between devices, on_device(): key_piece = lax.all_gather(keys_here, 'blk', axis=1, tiled=True)  50.1 us
    all_gather x1, waiting for transfers between devices, on_device(): lax.all_gather(w_out, 'blk', axis=0, tiled=True)  47.9 us
    all_gather x1, waiting for transfers between devices, on_device(): value_piece = lax.all_gather(values_here, 'blk', axis=1, tiled=True)  47.1 us
    reduce_scatter x1, waiting for transfers between devices, on_device(): lax.psum_scatter(group_terms.astype(jnp.bfloat16), 'head', scatter_dimens...  32.2 us
    all_gather x1, blocking collectives, on_device(): lax.all_gather(normed, 'head', axis=1, tiled=True)  26.5 us
    all_to_all x1, starting transfers between devices, trees_build(): lax.all_to_all(jnp.stack(lax.axis_size(peer_axis) * [arr_in]), peer_axis,...  7.63 us
    all_gather x1, blocking collectives, carried_in(): gathered = lax.all_gather(array.astype(jnp.bfloat16), axis)  7.15 us
  transfers between devices with their start and end apart: 5, of which 5 were waited for; matrix products, arithmetic and copies ran while one was open for 5% of the time, Pallas kernels for 0%

profile of v1, /device:TPU:1, one launch (start us, length us, event | category | flops | bytes accessed | tf_op | source)
XLA Modules:
  0.0 340.4 jit_solution(16684380612365796021)
XLA Ops:
  6.5 5.1 %stack.2 = bf16[16,192,3,384]{3,1,2,0:T(8,128)(2,1)} broadcast(bf16[192,3,384]{2,0,1:T(8,128)(2,1)} %param.14), dimensions={1,2,3} | broadcast | bytes 7520256 | tf_op jit(solution)/shard_map/stack | solution.py:12
  11.6 7.6 %all-to-all-start = ((bf16[16,192,3,384]{3,1,2,0:T(8,128)(2,1)}), bf16[16,192,3,384]{3,1,2,0:T(8,128)(2,1)}, u32[]{:S(2)}, u32[]{:S(2)}) async-start(bf16[16,192,3,384]{3,1,2,0:T(8,128)(2,1)} %stack.2), calls=%async_computation | async-start | bytes 14155776 | tf_op jit(solution)/shard_map/all_to_all | solution.py:12
  19.2 0.0 all-gather.4.cloned.1.call-start
  19.3 0.0 copy-start.4
  19.3 3.2 reshape.445
  23.1 0.0 copy-done.4
  23.1 0.1 reduce_sum.100
  23.3 0.2 multiply_reduce_fusion.2
  23.5 1.8 fusion.1
  25.3 0.1 add_convert_fusion
  25.5 26.5 %all_gather.16 = bf16[1,128,3072]{2,1,0:T(8,128)(2,1)S(1)} all-gather(bf16[1,16,3072]{2,1,0:T(8,128)(2,1)S(1)} %add_convert_fusion), channel_id=1, replica_groups=mesh['step'=2,'head'=8,'blk'=16] {'head'}, dimensions={1}, use_global_device_ids=true | all-gather | bytes 884736 | tf_op jit(solution)/shard_map/all_gather | solution.py:58
  51.9 71.2 %all-to-all-done = bf16[16,192,3,384]{3,1,2,0:T(8,128)(2,1)} async-done(((bf16[16,192,3,384]{3,1,2,0:T(8,128)(2,1)}), bf16[16,192,3,384]{3,1,2,0:T(8,128)(2,1)}, u32[]{:S(2)}, u32[]{:S(2)}) %all-to-all-start) | async-done | bytes 7077920 | tf_op jit(solution)/shard_map/all_to_all | solution.py:12
  123.1 3.9 %copy.20 = bf16[16,192,3,384]{3,1,0,2:T(8,128)(2,1)S(1)} copy(bf16[16,192,3,384]{3,1,2,0:T(8,128)(2,1)} %all-to-all-done) | data formatting | bytes 14155776 | tf_op jit(solution)/shard_map/all_to_all | solution.py:12
  127.0 1.2 convolution_bitcast_fusion
  128.2 0.0 copy-start.9
  128.2 0.0 copy-start.10
  128.3 0.1 copy.23
  128.5 0.4 copy-done.9
  128.9 0.7 multiply_convert_fusion
  129.6 0.0 all-gather.4.cloned.1.call-update
  129.6 0.0 all-gather.6.cloned.1.call-start
  129.7 0.7 copy.25
  130.4 0.0 all-gather.6.cloned.1.call-update
  130.5 0.0 all-gather.8.cloned.1.call-start
  130.5 0.7 all-gather.8.cloned.1.call-update
  131.2 0.0 reduce-scatter.2.cloned.1.call-start
  131.2 0.1 copy.21
  131.5 0.0 copy-done.10
  131.5 0.1 multiply_convert_fusion.1
  131.6 50.1 %all-gather.4.cloned.1.call-done = bf16[1,2048,6,64]{1,3,2,0:T(8,128)(2,1)} async-done(((bf16[1,128,6,64]{1,3,2,0:T(8,128)(2,1)}), bf16[1,2048,6,64]{1,3,2,0:T(8,128)(2,1)}) %all-gather.4.cloned.1.call-update) | async-done | bytes 1572880 | tf_op jit(solution)/shard_map/all_gather | solution.py:81
  181.7 1.6 fusion.41
  183.3 0.0 copy-done.5
  183.3 0.5 fusion.38
  183.8 0.0 copy-start.2
  183.8 0.5 fusion.39
  184.3 0.5 fusion.40
  184.8 0.1 copy-done.2
  184.9 0.9 fusion.7
  185.8 0.1 copy-done
  185.9 0.9 fusion.3
  186.9 47.1 %all-gather.6.cloned.1.call-done = bf16[1,2048,6,64]{1,3,2,0:T(8,128)(2,1)} async-done(((bf16[1,128,6,64]{1,3,2,0:T(8,128)(2,1)}), bf16[1,2048,6,64]{1,3,2,0:T(8,128)(2,1)}) %all-gather.6.cloned.1.call-update) | async-done | bytes 1572880 | tf_op jit(solution)/shard_map/all_gather | solution.py:82
  233.9 1.6 fusion.14
  235.5 0.0 copy-start.6
  235.5 0.0 copy-done.1
  235.5 1.6 fusion.13
  237.1 0.0 copy-start.3
  237.1 0.0 copy-done.6
  237.1 0.5 fusion.12
  237.6 0.9 copy-done.3
  238.5 0.5 fusion.15
  239.0 47.9 %all-gather.8.cloned.1.call-done = bf16[384,3072]{1,0:T(8,128)(2,1)} async-done(((bf16[24,3072]{1,0:T(8,128)(2,1)}), bf16[384,3072]{1,0:T(8,128)(2,1)}) %all-gather.8.cloned.1.call-update) | async-done | bytes 2359312 | tf_op jit(solution)/shard_map/all_gather | solution.py:111
  286.9 3.2 fusion
  290.0 0.0 reduce-scatter.2.cloned.1.call-update
  290.7 0.0 copy-done.11
  290.7 0.7 fusion.30
  291.4 32.2 %reduce-scatter.2.cloned.1.call-done = bf16[1,16,3072]{2,1,0:T(8,128)(2,1)} async-done(((bf16[1,128,3072]{2,1,0:T(8,128)(2,1)}), bf16[1,16,3072]{2,1,0:T(8,128)(2,1)}) %reduce-scatter.2.cloned.1.call-update) | async-done | bytes 98320 | tf_op jit(solution)/shard_map/reduce_scatter | solution.py:114
  323.6 1.6 fusion.26
  325.2 0.0 copy-start.7
  325.2 0.0 copy-start.8
  325.2 7.2 %all_gather.20 = bf16[2,16,3072]{2,1,0:T(8,128)(2,1)S(1)} all-gather(bf16[1,16,3072]{2,1,0:T(8,128)(2,1)S(1)} %fusion.26), channel_id=1, replica_groups=mesh['step'=2,'head'=8,'blk'=16] {'step'}, dimensions={0}, use_global_device_ids=true | all-gather | bytes 294912 | tf_op jit(solution)/shard_map/all_gather | solution.py:22
  332.4 0.1 while.10
  332.5 0.0 copy-done.7
  332.5 0.0 copy-done.8
  332.5 1.4 fusion.25
  (22 shorter events, 0.3 us)
Async XLA Ops:
  11.6 111.5 %all-to-all-start = ((bf16[16,192,3,384]{3,1,2,0:T(8,128)(2,1)}), bf16[16,192,3,384]{3,1,2,0:T(8,128)(2,1)}, u32[]{:S(2)}, u32[]{:S(2)}) async-start(bf16[16,192,3,384]{3,1,2,0:T(8,128)(2,1)} %stack.2), calls=%async_computation | async-start | bytes 14155776 | tf_op jit(solution)/shard_map/all_to_all | solution.py:12
  19.2 162.4 %all-gather.4.cloned.1.call-start = ((), (), s32[]{:S(2)}) async-start(), calls=%async_computation.2 | async-start | bytes 1671168 | tf_op jit(solution)/shard_map/all_gather | solution.py:81
  19.3 3.8 %copy-start.4 = (f32[1,16,3072]{2,1,0:T(8,128)S(1)}, f32[1,16,3072]{2,1,0:T(8,128)}, u32[]{:S(2)}) copy-start(f32[1,16,3072]{2,1,0:T(8,128)} %param.12) | copy-start | bytes 589828
  128.2 0.7 copy-start.9
  128.2 3.2 copy-start.10
  129.6 104.3 %all-gather.6.cloned.1.call-start = ((), (), s32[]{:S(2)}) async-start(), calls=%async_computation.3 | async-start | bytes 1671168 | tf_op jit(solution)/shard_map/all_gather | solution.py:82
  130.5 156.4 %all-gather.8.cloned.1.call-start = ((), (), s32[]{:S(2)}) async-start(), calls=%async_computation.4 | async-start | bytes 2506752 | tf_op jit(solution)/shard_map/all_gather | solution.py:111
  131.2 192.4 %reduce-scatter.2.cloned.1.call-start = ((), (), s32[]{:S(2)}) async-start(), calls=%async_computation.5 | async-start | bytes 884736 | tf_op jit(solution)/shard_map/reduce_scatter | solution.py:114
  181.7 1.6 copy-start.5
  183.8 1.2 copy-start.2
  184.8 1.2 copy-start
  233.9 1.6 copy-start.1
  235.5 1.6 copy-start.6
  237.1 1.4 copy-start.3
  286.9 3.9 %copy-start.11 = (f32[50]{0:T(128)S(1)}, f32[50]{0:T(128)}, u32[]{:S(2)}) copy-start(f32[50]{0:T(128)} %param.20) | copy-start | bytes 604
  325.2 7.3 %copy-start.7 = (bf16[1,16,3072]{2,1,0:T(8,128)(2,1)S(1)}, bf16[1,16,3072]{2,1,0:T(8,128)(2,1)}, u32[]{:S(2)}) copy-start(bf16[1,16,3072]{2,1,0:T(8,128)(2,1)} %reduce-scatter.2.cloned.1.call-done) | copy-start | bytes 294916
  325.2 7.3 %copy-start.8 = (f32[16,3072]{1,0:T(8,128)S(1)}, f32[16,3072]{1,0:T(8,128)}, u32[]{:S(2)}) copy-start(f32[16,3072]{1,0:T(8,128)} %param.13) | copy-start | bytes 589828
Sparse Core Ops, SparseCore 0:
  129.7 51.8 all-gather.3
  184.1 49.8 all-gather.5
  236.4 50.4 all-gather.7
  290.2 33.3 reduce-scatter.1
